TPU v7x, 32 devices: a whole 2x2x4 slice. The times are simulated.
32 devices in a mesh: sweep: 2 (over y), rows: 8 (over z, x), coef: 2 (over core).
Axes of the slice: x: 2, y: 2, z: 4, core: 2. Of those that a mesh axis runs over, the one named last changes fastest.
Arguments:
- snapshots: bfloat16 [8192, 128], P(('sweep', 'rows')), parts along dimension 0, may hold values from -34 to 34
- panel_order: int32 [8192], P(('sweep', 'rows')), parts along dimension 0, may hold values from 0 to 511, as said below
- tile_values: bfloat16 [16, 16, 4, 256, 256], P(('sweep', 'coef'), 'rows'), parts along dimension 0, may hold values from -0.1875 to 0.1875
- self_coef: float32 [16, 4096], P(('sweep', 'coef'), 'rows'), parts along dimension 0, may hold values from 0.5 to 4
- col_index: int32 [16, 16, 4], P(('sweep', 'coef'), 'rows'), parts along dimension 0, may hold values from 0 to 15, as said below
- frequency: float32 [2], P('sweep'), parts along dimension 0, may hold values from -0.95 to 0.95
Outputs:
- sampled_image: bfloat16 [8192, 128], P(('sweep', 'rows'), 'coef'), parts along dimension 0
- projected: float32 [16, 128, 128], P(('sweep', 'coef')), parts along dimension 0
There are 2 independent parts, one for each index of `sweep`. A program takes and returns all parts, laid end to end along the dimension named above; each array names one. Nothing has to cross between parts.
Inputs may be any that keep to these rules, and one draw needn't show every extreme that they name: `panel_order`: each aligned block of 512 entries starting at a multiple of 512 is a permutation of 0 to 511. `col_index`: entry [k, b, n] is the column block of tile n of block row b of operator k; entry n = 0 is b itself, entry n = 1 lies exactly 2 blocks from b, and every entry lies within 2 blocks of b.
All inputs are finite; a program needn't handle non-finite values.
Results may differ from a plain program's by a relative error of at most 0.0095.
Values may be sent and summed in bfloat16 or wider, within the bound.
A program may use at most 64 MiB of HBM per device.

v0:
```python
from functools import partial

import jax
import jax.numpy as jnp
from jax import lax
from jax.sharding import PartitionSpec as P

K = 8


def extended(x, sides, width):
    for axis, dim in sides:
        count, length = (lax.axis_size(axis), x.shape[dim])
        up = [(i, (i + 1) % count) for i in range(count - 1)]
        down = [(j, i) for i, j in up]
        last = lax.slice_in_dim(x, length - width, length, axis=dim)
        first = lax.slice_in_dim(x, 0, width, axis=dim)
        before = lax.ppermute(last, axis, up)
        after = lax.ppermute(first, axis, down)
        x = jnp.concatenate([before, x, after], axis=dim)
    return x


def chebyshev(point):
    values_list = [jnp.ones_like(point), point]
    for degree in range(2, K):
        values_list.append(2.0 * point * values_list[-1] - values_list[-2])
    return jnp.stack(values_list[:K])


def sandwich(factor, matrix):
    inner = jax.scipy.linalg.solve_triangular(factor, matrix, lower=True)
    return jax.scipy.linalg.solve_triangular(factor, inner.T, lower=True).T


def gram_of(panels_here):
    return lax.dot_general(
        panels_here, panels_here, (((0,), (0,)), ((), ())), preferred_element_type=jnp.float32
    )


def local(snapshots, panel_order, tile_values, self_coef, col_index, frequency):
    slab_rows, columns = snapshots.shape
    local_ops, blocks, per_row, tile_rows = tile_values.shape[:4]
    ordered = jnp.take(snapshots, panel_order, axis=0)
    padded = extended(ordered, (("rows", 0),), slab_rows)
    panels = padded.reshape(3 * blocks, tile_rows, columns)
    first_block = lax.axis_index("rows") * blocks - blocks
    picked = jnp.take(panels, col_index - first_block, axis=0)
    near_field = jnp.einsum(
        "kbnij,kbnjr->kbir", tile_values, picked, preferred_element_type=jnp.float32
    )
    images = (
        near_field.reshape(local_ops, slab_rows, columns)
        + self_coef[:, :, None] * ordered.astype(jnp.float32)[None]
    ).astype(jnp.bfloat16)
    weights = lax.dynamic_slice_in_dim(
        chebyshev(frequency[0]), lax.axis_index("coef") * local_ops, local_ops
    )
    weighted = jnp.sum(weights[:, None, None] * images.astype(jnp.float32), axis=0)
    sampled_image = lax.psum_scatter(weighted, "coef", scatter_dimension=1, tiled=True).astype(
        jnp.bfloat16
    )
    gram_local = gram_of(ordered)
    projection_terms = jnp.einsum(
        "pr,kpq->krq", ordered, images, preferred_element_type=jnp.float32
    )
    gram_total = lax.psum(gram_local, "rows")
    factor = jnp.linalg.cholesky(gram_total)
    projection_total = lax.psum(projection_terms, "rows")
    projected = jax.vmap(partial(sandwich, factor))(projection_total)
    return (sampled_image, projected)


def solution(mesh):
    placed = (
        P(("sweep", "rows"), None),
        P(("sweep", "rows")),
        P(("sweep", "coef"), "rows", None, None, None),
        P(("sweep", "coef"), "rows"),
        P(("sweep", "coef"), "rows", None),
        P("sweep"),
    )
    return jax.shard_map(
        local,
        mesh=mesh,
        in_specs=placed,
        out_specs=(P(("sweep", "rows"), "coef"), P(("sweep", "coef"), None, None)),
        check_vma=False,
    )
```

profile of v0, /device:TPU:0, one launch (start us, length us, event | category | flops | bytes accessed | tf_op | source)
XLA Modules:
  0.0 142.1 jit_solution(5365914901657669841)
XLA Ops:
  8.0 0.0 copy-start
  8.0 0.0 copy-start.2
  8.0 0.0 copy-start.1
  8.0 0.0 all-reduce.3.cloned.1.call-start
  8.1 0.7 compare_select_fusion.1
  8.8 0.7 compare_and_fusion.1
  9.5 0.0 copy-done
  9.5 1.3 gather_fusion
  10.8 0.1 fusion.16
  11.0 4.8 %collective-permute-start = (bf16[512,128]{1,0:T(8,128)(2,1)S(1)}, bf16[512,128]{1,0:T(8,128)(2,1)S(1)}, u32[]{:S(2)}, u32[]{:S(2)}) collective-permute-start(bf16[512,128]{1,0:T(8,128)(2,1)S(1)} %get-tuple-element.16), channel_id=1, source_target_pairs={{0,2},{2,4},{4,6},{6,8},{8,10},{10,12},{12,14},{1,3},{3,5},{5,7},{... | collective-permute-start | bytes 393224 | tf_op jit(solution)/shard_map/ppermute | solution.py:18
  15.8 1.3 collective-permute-start.1
  17.2 0.9 fusion.17
  18.0 0.1 copy.58
  18.2 0.0 copy-done.2
  18.9 0.1 reshape.71
  19.0 0.0 copy-done.1
  19.0 0.1 stack.27
  19.1 0.1 dynamic_slice.3
  19.1 0.0 collective-permute-done
  19.2 3.5 %collective-permute-done.1 = bf16[512,128]{1,0:T(8,128)(2,1)S(1)} collective-permute-done((bf16[512,128]{1,0:T(8,128)(2,1)S(1)}, bf16[512,128]{1,0:T(8,128)(2,1)S(1)}, u32[]{:S(2)}, u32[]{:S(2)}) %collective-permute-start.1) | collective-permute-done | bytes 131104 | tf_op jit(solution)/shard_map/ppermute | solution.py:19
  22.7 1.0 gather_fusion.1
  23.7 2.9 %copy.57 = bf16[32,256,128]{1,2,0:T(8,128)(2,1)} copy(bf16[32,256,128]{2,1,0:T(8,128)(2,1)S(1)} %gather_fusion.1) | data formatting | bytes 4194304 | tf_op jit(solution)/shard_map/jit(_take)/gather | solution.py:49
  26.6 4.4 %multiply_reduce_fusion = (f32[2,256,128]{1,2,0:T(8,128)S(1)}, f32[4,2,256,128]{2,3,1,0:T(8,128)S(1)}) fusion(f32[2,256,128]{1,2,0:T(8,128)S(1)} %select_convert_fusion, f32[4,2,256]{2,1,0:T(2,128)S(1)} %mul.73, f32[4]{0:T(128)S(1)} %dynamic_slice.3, bf16[4,2,4,256,256]{4,3,2,1,0:T(8,128)(2,1)} %param.10, bf16[4,2,4,256,128]{3,4,2,1,0:T(8,128)(2,1)} %bitcast.72, ...), kind=kOutput, calls=%fused_computation.11 | convolution fusion | flops 539426816 | bytes 7872560 | tf_op jit(solution)/shard_map/kbnij,kbnjr->kbir/dot_general | solution.py:50
  31.0 0.3 copy.62
  31.3 0.3 fusion.6
  31.7 1.0 convolution_bitcast_fusion
  32.7 0.0 all-reduce.3.cloned.1.call-update
  32.7 0.0 reduce-scatter.4.cloned.1.call-start
  32.8 0.1 copy.59
  32.9 0.8 copy.79
  33.7 0.0 reduce-scatter.4.cloned.1.call-update
  33.8 71.5 %all-reduce.3.cloned.1.call-done = (f32[4,128,128]{1,2,0:T(8,128)}, f32[128,128]{0,1:T(8,128)}) async-done(((f32[4,128,128]{1,2,0:T(8,128)}, f32[128,128]{0,1:T(8,128)}), (f32[4,128,128]{1,2,0:T(8,128)}, f32[128,128]{0,1:T(8,128)})) %all-reduce.3.cloned.1.call-update) | async-done | bytes 327696 | tf_op jit(solution)/shard_map/psum | solution.py:70
  105.3 0.9 copy.61
  106.2 0.9 fusion.14
  107.0 11.7 %cholesky.18 = f32[128,128]{1,0:T(8,128)S(1)} custom-call(f32[128,128]{1,0:T(8,128)S(1)} %fusion.14), custom_call_target="Cholesky" | custom-call | tf_op jit(solution)/shard_map/jit(cholesky)/cholesky | solution.py:69
  118.8 0.6 compare_reduce_fusion
  119.4 0.7 fusion.11
  120.1 9.8 %custom-call.8 = f32[1,128,128]{1,2,0:T(8,128)S(1)} custom-call(f32[1,128,128]{2,1,0:T(8,128)S(1)} %fusion.11), custom_call_target="InvertDiagBlocksLowerTriangular" | custom-call | tf_op jit(solution)/shard_map/vmap(jit(_solve_triangular))/triangular_solve | solution.py:33
  129.9 1.1 copy.88
  131.0 0.4 convolution_bitcast_fusion.2
  131.5 0.2 copy.87
  131.6 0.4 convolution_bitcast_fusion.1
  132.1 0.8 copy.71
  132.9 0.0 reduce-scatter.4.cloned.1.call-done
  132.9 1.0 copy.80
  133.9 0.7 copy.70
  (8 shorter events, 0.1 us)
Async XLA Ops:
  8.0 1.5 %copy-start = (bf16[512,128]{1,0:T(8,128)(2,1)S(1)}, bf16[512,128]{1,0:T(8,128)(2,1)}, u32[]{:S(2)}) copy-start(bf16[512,128]{1,0:T(8,128)(2,1)} %param.8) | copy-start | bytes 393220
  8.0 10.2 %copy-start.2 = (s32[4,2,4]{2,1,0:T(2,128)S(1)}, s32[4,2,4]{2,1,0:T(2,128)}, u32[]{:S(2)}) copy-start(s32[4,2,4]{2,1,0:T(2,128)} %param.12) | copy-start | bytes 388
  8.0 10.9 %copy-start.1 = (f32[4,512]{1,0:T(4,128)S(1)}, f32[4,512]{1,0:T(4,128)}, u32[]{:S(2)}) copy-start(f32[4,512]{1,0:T(4,128)} %param.11) | copy-start | bytes 24580
  8.0 97.2 %all-reduce.3.cloned.1.call-start = ((), (), s32[]{:S(2)}) async-start(), calls=%async_computation.2 | async-start | bytes 655360 | tf_op jit(solution)/shard_map/psum | solution.py:70
  11.0 8.2 %collective-permute-start = (bf16[512,128]{1,0:T(8,128)(2,1)S(1)}, bf16[512,128]{1,0:T(8,128)(2,1)S(1)}, u32[]{:S(2)}, u32[]{:S(2)}) collective-permute-start(bf16[512,128]{1,0:T(8,128)(2,1)S(1)} %get-tuple-element.16), channel_id=1, source_target_pairs={{0,2},{2,4},{4,6},{6,8},{8,10},{10,12},{12,14},{1,3},{3,5},{5,7},{... | collective-permute-start | bytes 393224 | tf_op jit(solution)/shard_map/ppermute | solution.py:18
  15.8 6.9 %collective-permute-start.1 = (bf16[512,128]{1,0:T(8,128)(2,1)S(1)}, bf16[512,128]{1,0:T(8,128)(2,1)S(1)}, u32[]{:S(2)}, u32[]{:S(2)}) collective-permute-start(bf16[512,128]{1,0:T(8,128)(2,1)S(1)} %get-tuple-element.16), channel_id=1, source_target_pairs={{2,0},{4,2},{6,4},{8,6},{10,8},{12,10},{14,12},{3,1},{5,3},{7,5},{... | collective-permute-start | bytes 393224 | tf_op jit(solution)/shard_map/ppermute | solution.py:19
  32.7 100.2 %reduce-scatter.4.cloned.1.call-start = ((), (), s32[]{:S(2)}) async-start(), calls=%async_computation.1 | async-start | bytes 393216
Sparse Core Ops, SparseCore 0:
  32.9 72.3 all-reduce.2
Sparse Core Ops, SparseCore 1:
  35.4 8.8 reduce-scatter.3
where the time goes:
time: 142 us
  waiting for transfers between devices  75.1 us (53%)
  other arithmetic  25.7 us (18%)
  between operations  16.4 us (12%)
  local copies, waits for them, and re-layouts  11.7 us (8%)
  matrix products  7.11 us (5%)
  starting transfers between devices  6.22 us (4%)
    psum x1, waiting for transfers between devices, local(): projection_total = lax.psum(projection_terms, 'rows')  71.5 us
    another operation x3, other arithmetic, local(): factor = jnp.linalg.cholesky(gram_total)  12.4 us
    another operation x2, other arithmetic, sandwich(): return jax.scipy.linalg.solve_triangular(factor, inner.T, lower=True).T  10.5 us
    ppermute x1, starting transfers between devices, extended(): before = lax.ppermute(last, axis, up)  4.85 us
    dot_general x1, matrix products, local(): jnp.einsum('kbnij,kbnjr->kbir', tile_values, picked, preferred_element_ty...  4.37 us
    gather x2, local copies, waits for them, and re-layouts, local(): picked = jnp.take(panels, col_index - first_block, axis=0)  3.87 us
    ppermute x1, waiting for transfers between devices, extended(): after = lax.ppermute(first, axis, down)  3.54 us
    unnamed x10, local copies, waits for them, and re-layouts  3.44 us
  transfers between devices with their start and end apart: 4, of which 2 were waited for; matrix products, arithmetic and copies ran while one was open for 21% of the time, Pallas kernels for 0%

commit v1 on v0

v1 whole, which is shorter than its diff:
```python
import functools

import jax
import jax.numpy as jnp
from jax import lax
from jax.experimental import pallas as pl
from jax.experimental.pallas import tpu as pltpu
from jax.sharding import PartitionSpec as P

K = 8
MESH = pl.DeviceIdType.MESH
HIGHEST = lax.Precision.HIGHEST
F32 = jnp.float32


def chebyshev(point):
    values = [jnp.float32(1.0), point]
    for _ in range(2, K):
        values.append(2.0 * point * values[-1] - values[-2])
    return values


def inverse_factor(a, w_ref):
    n = a.shape[0]
    row = lax.broadcasted_iota(jnp.int32, (n, n), 0)
    column = lax.broadcasted_iota(jnp.int32, (n, n), 1)
    right = jnp.where(row == column, 1.0, 0.0).astype(F32)
    rows8 = lax.broadcasted_iota(jnp.int32, (8, n), 0)
    for r0 in range(0, n, 8):
        rest = n - r0 - 8
        sa, sr, ta, tr = a[:8], right[:8], a[8:], right[8:]
        sc = [jnp.broadcast_to(sa[:, r0 + j : r0 + j + 1], (8, n)) for j in range(8)]
        if rest:
            tc = [jnp.broadcast_to(ta[:, r0 + j : r0 + j + 1], (rest, n)) for j in range(8)]
        scale = jnp.zeros((8, n), F32)
        for j in range(8):
            pivot = jnp.broadcast_to(sc[j][j : j + 1], (8, n))
            inverse = 1.0 / pivot
            factors = jnp.where(rows8 > j, sc[j] * inverse, 0.0)
            y = lax.rsqrt(pivot)
            y = y * (1.5 - 0.5 * pivot * y * y)
            scale = jnp.where(rows8 == j, y, scale)
            row_a, row_r = sa[j : j + 1], sr[j : j + 1]
            heads = [sc[i][j : j + 1] for i in range(8)]
            for i in range(j + 1, 8):
                sc[i] = sc[i] - factors * heads[i]
            sa = sa - factors * row_a
            sr = sr - factors * row_r
            if rest:
                below = tc[j] * inverse[:1]
                for i in range(j + 1, 8):
                    tc[i] = tc[i] - below * heads[i]
                ta = ta - below * row_a
                tr = tr - below * row_r
        w_ref[r0 : r0 + 8, :] = sr * scale
        a, right = ta, tr


def kernel(
    n, snap_ref, order_ref, tiles_ref, coef_ref, col_ref, freq_ref,
    sampled_ref, projected_ref,
    tiles, panels, acc, gsend, grecv, gsum, gall, w, wt, psend, precv, tsend, tall, wsend, wrecv,
    tile_sem, gs_sem, gr_sem, as_sem, ar_sem, hs_sem, hr_sem, fs_sem, fr_sem,
    ps_sem, pr_sem, ts_sem, tr_sem, ws_sem, wr_sem,
):
    me = lax.axis_index("rows")
    half = lax.axis_index("coef")
    other = 1 - half
    ops, blocks, per_row, tile_rows = tiles.shape[:4]
    slab, rank = snap_ref.shape
    per_op = n // ops
    t_rows = rank // per_op

    def peers(step):
        if n <= 8:
            for d in range(1, n):
                step(d, lax.rem(me + d, n))
        else:
            @pl.loop(1, n)
            def _(d):
                step(d, lax.rem(me + d, n))

    load = [
        pltpu.make_async_copy(tiles_ref.at[k], tiles.at[k], tile_sem.at[k]) for k in range(ops)
    ]
    for copy in load:
        copy.start()

    barrier = pltpu.get_barrier_semaphore()
    peers(lambda d, peer: pl.semaphore_signal(
        barrier, inc=1, device_id={"rows": peer}, device_id_type=MESH))
    pl.semaphore_signal(barrier, inc=1, device_id={"coef": other}, device_id_type=MESH)

    snap = snap_ref[...]
    snap_t = snap.astype(F32).T.astype(jnp.bfloat16)
    gram = jnp.dot(snap_t, snap, preferred_element_type=F32)
    place = lax.broadcasted_iota(jnp.int32, (slab, slab), 0)
    one_hot = jnp.where(place == order_ref[...], 1.0, 0.0).astype(jnp.bfloat16)
    ordered_t = jnp.dot(snap_t, one_hot, preferred_element_type=F32)
    ordered = ordered_t.T
    for b in range(blocks):
        panels[blocks + b] = ordered[b * tile_rows : (b + 1) * tile_rows].astype(jnp.bfloat16)
    g_rows = rank // n
    for i in range(n):
        gsend[i] = gram[i * g_rows : (i + 1) * g_rows]

    @pl.when(me == 0)
    def _():
        for b in range(blocks):
            panels[b] = jnp.zeros(panels.shape[1:], panels.dtype)

    @pl.when(me == n - 1)
    def _():
        for b in range(blocks):
            panels[2 * blocks + b] = jnp.zeros(panels.shape[1:], panels.dtype)

    pl.semaphore_wait(barrier, n)

    def gram_part(slot, source, peer):
        return pltpu.make_async_remote_copy(
            src_ref=gsend.at[peer], dst_ref=grecv.at[source],
            send_sem=gs_sem.at[slot], recv_sem=gr_sem.at[source],
            device_id={"rows": peer}, device_id_type=MESH)

    peers(lambda d, peer: gram_part(d, me, peer).start())

    share = blocks // 2
    mine = half * share

    def halo(way, first_block, peer, to):
        return pltpu.make_async_remote_copy(
            src_ref=panels.at[pl.ds(first_block, share)], dst_ref=panels.at[pl.ds(to, share)],
            send_sem=hs_sem.at[way], recv_sem=hr_sem.at[way],
            device_id={"rows": peer}, device_id_type=MESH)

    def forward(way, base):
        place = pl.ds(base + mine, share)
        return pltpu.make_async_remote_copy(
            src_ref=panels.at[place], dst_ref=panels.at[place],
            send_sem=fs_sem.at[way], recv_sem=fr_sem.at[way],
            device_id={"coef": other}, device_id_type=MESH)

    up = halo(0, blocks + mine, jnp.minimum(me + 1, n - 1), mine)
    down = halo(1, blocks + mine, jnp.maximum(me - 1, 0), 2 * blocks + mine)

    @pl.when(me < n - 1)
    def _():
        up.start()

    @pl.when(me > 0)
    def _():
        down.start()

    coef_t = jnp.concatenate([coef_ref[...]] * (8 // ops), axis=0).T
    for k in range(ops):
        load[k].wait()
        for b in range(blocks):
            here = slice(b * tile_rows, (b + 1) * tile_rows)
            acc[k, here] = coef_t[here, k : k + 1] * ordered[here] + jnp.dot(
                tiles[k, b, 0], panels[blocks + b], preferred_element_type=F32)

    grecv[me] = gsend[me]
    peers(lambda d, peer: gram_part(d, peer, peer).wait_recv())
    gsum[...] = jnp.sum(grecv[...], axis=0)
    gall[me] = gsum[...]

    def gram_all(slot, source, peer):
        return pltpu.make_async_remote_copy(
            src_ref=gsum, dst_ref=gall.at[source],
            send_sem=as_sem.at[slot], recv_sem=ar_sem.at[source],
            device_id={"rows": peer}, device_id_type=MESH)

    peers(lambda d, peer: gram_all(d, me, peer).start())

    @pl.when(me > 0)
    def _():
        up.wait_recv()
        forward(0, 0).start()

    @pl.when(me < n - 1)
    def _():
        down.wait_recv()
        forward(1, 2 * blocks).start()

    @pl.when(me > 0)
    def _():
        forward(0, 0).wait()

    @pl.when(me < n - 1)
    def _():
        forward(1, 2 * blocks).wait()

    first = me * blocks - blocks
    weights = chebyshev(freq_ref[0])
    ordered_b = ordered_t.astype(jnp.bfloat16)
    weighted = jnp.zeros((slab, rank), F32)
    for k in range(ops):
        parts = []
        for b in range(blocks):
            here = slice(b * tile_rows, (b + 1) * tile_rows)
            total = acc[k, here]
            for j in range(1, per_row):
                at = jnp.clip(col_ref[k, b, j] - first, 0, 3 * blocks - 1)
                total = total + jnp.dot(tiles[k, b, j], panels[at], preferred_element_type=F32)
            parts.append(total.astype(jnp.bfloat16))
        image = jnp.concatenate(parts, axis=0)
        weight = jnp.where(half == 0, weights[k], weights[k + ops])
        weighted = weighted + weight * image.astype(F32)
        psend[k] = jnp.dot(ordered_b, image, preferred_element_type=F32)
    wsend[...] = weighted

    def projection_part(slot, source, peer):
        return pltpu.make_async_remote_copy(
            src_ref=psend.at[peer // per_op], dst_ref=precv.at[source],
            send_sem=ps_sem.at[slot], recv_sem=pr_sem.at[source],
            device_id={"rows": peer}, device_id_type=MESH)

    peers(lambda d, peer: projection_part(d, me, peer).start())
    swap = pltpu.make_async_remote_copy(
        src_ref=wsend, dst_ref=wrecv, send_sem=ws_sem, recv_sem=wr_sem,
        device_id={"coef": other}, device_id_type=MESH)
    swap.start()
    precv[me] = psend[me // per_op]

    peers(lambda d, peer: gram_all(d, peer, peer).wait_recv())
    inverse_factor(jnp.concatenate([gall[i] for i in range(n)], axis=0), w)
    for i in range(per_op):
        wt[i] = w[i * t_rows : (i + 1) * t_rows, :]

    swap.wait()
    both = (wsend[...] + wrecv[...]).T
    width = rank // 2
    sampled_ref[...] = jnp.where(half == 0, both[:width], both[width:]).astype(jnp.bfloat16)

    peers(lambda d, peer: projection_part(d, peer, peer).wait_recv())
    total = precv[0]
    if n <= 8:
        for i in range(1, n):
            total = total + precv[i]
    else:
        total = lax.fori_loop(1, n, lambda i, t: t + precv[i], total)
    inner = jnp.dot(wt[lax.rem(me, per_op)], total, preferred_element_type=F32, precision=HIGHEST)
    tsend[...] = lax.dot_general(
        inner, w[...], (((1,), (1,)), ((), ())), preferred_element_type=F32, precision=HIGHEST)
    tall[me] = tsend[...]

    def result_part(slot, source, peer):
        return pltpu.make_async_remote_copy(
            src_ref=tsend, dst_ref=tall.at[source],
            send_sem=ts_sem.at[slot], recv_sem=tr_sem.at[source],
            device_id={"rows": peer}, device_id_type=MESH)

    peers(lambda d, peer: result_part(d, me, peer).start())

    def sent(d, peer):
        gram_part(d, me, peer).wait_send()
        gram_all(d, me, peer).wait_send()
        projection_part(d, me, peer).wait_send()

    peers(sent)

    @pl.when(me < n - 1)
    def _():
        up.wait_send()

    @pl.when(me > 0)
    def _():
        down.wait_send()

    peers(lambda d, peer: result_part(d, peer, peer).wait_recv())
    for i in range(n):
        k, h = divmod(i, per_op)
        projected_ref[k, h * t_rows : (h + 1) * t_rows, :] = tall[i]
    peers(lambda d, peer: result_part(d, me, peer).wait_send())


def local(n, snapshots, panel_order, tile_values, self_coef, col_index, frequency):
    slab, rank = snapshots.shape
    ops, blocks, per_row, tile_rows = tile_values.shape[:4]
    t_rows = rank * ops // n
    vmem = pl.BlockSpec(memory_space=pltpu.VMEM)
    smem = pl.BlockSpec(memory_space=pltpu.SMEM)
    dma = pltpu.SemaphoreType.DMA
    sampled_t, projected = pl.pallas_call(
        functools.partial(kernel, n),
        out_shape=(
            jax.ShapeDtypeStruct((rank // 2, slab), jnp.bfloat16),
            jax.ShapeDtypeStruct((ops, rank, rank), F32),
        ),
        in_specs=[vmem, vmem, pl.BlockSpec(memory_space=pl.ANY), vmem, smem, smem],
        out_specs=(vmem, vmem),
        scratch_shapes=[
            pltpu.VMEM(tile_values.shape, jnp.bfloat16),
            pltpu.VMEM((3 * blocks, tile_rows, rank), jnp.bfloat16),
            pltpu.VMEM((ops, slab, rank), F32),
            pltpu.VMEM((n, rank // n, rank), F32),
            pltpu.VMEM((n, rank // n, rank), F32),
            pltpu.VMEM((rank // n, rank), F32),
            pltpu.VMEM((n, rank // n, rank), F32),
            pltpu.VMEM((rank, rank), F32),
            pltpu.VMEM((n // ops, t_rows, rank), F32),
            pltpu.VMEM((ops, rank, rank), F32),
            pltpu.VMEM((n, rank, rank), F32),
            pltpu.VMEM((t_rows, rank), F32),
            pltpu.VMEM((n, t_rows, rank), F32),
            pltpu.VMEM((slab, rank), F32),
            pltpu.VMEM((slab, rank), F32),
            dma((ops,)), dma((n,)), dma((n,)), dma((n,)), dma((n,)),
            dma((2,)), dma((2,)), dma((2,)), dma((2,)),
            dma((n,)), dma((n,)), dma((n,)), dma((n,)), dma, dma,
        ],
        compiler_params=pltpu.CompilerParams(
            collective_id=0, has_side_effects=True, vmem_limit_bytes=58 * 1024 * 1024),
        name="projection",
    )(snapshots, panel_order.reshape(1, slab), tile_values, self_coef, col_index, frequency)
    return sampled_t.T, projected


def solution(mesh):
    placed = (
        P(("sweep", "rows"), None),
        P(("sweep", "rows")),
        P(("sweep", "coef"), "rows", None, None, None),
        P(("sweep", "coef"), "rows"),
        P(("sweep", "coef"), "rows", None),
        P("sweep"),
    )
    return jax.shard_map(
        functools.partial(local, mesh.shape["rows"]),
        mesh=mesh,
        in_specs=placed,
        out_specs=(P(("sweep", "rows"), "coef"), P(("sweep", "coef"), None, None)),
        check_vma=False,
    )
```

time: 142 us -> 39.5 us (0.28)
  waiting for transfers between devices: 75.1 us -> 0 us
  Pallas kernels: 0 us -> 34.8 us
  other arithmetic: 25.7 us -> 0 us
  between operations: 16.4 us -> 1.29 us
  local copies, waits for them, and re-layouts: 11.7 us -> 3.14 us
  matrix products: 7.11 us -> 0 us
  starting transfers between devices: 6.22 us -> 0 us
    psum x1 -> x0, waiting for transfers between devices: 71.5 us -> none  [local(): projection_total = lax.psum(projection_terms, 'rows')]
    pallas_call x0 -> x1, Pallas kernels: none -> 34.8 us  [local(): pl.pallas_call(functools.partial(kernel, n), out_shape=(jax.ShapeDtypeStr...]
    another operation x5 -> x0, other arithmetic: 22.9 us -> none  [the longest x3 12.4 us: local(): factor = jnp.linalg.cholesky(gram_total)]
    dot_general x3 -> x0, matrix products: 6.27 us -> none  [the longest x1 4.37 us: local(): jnp.einsum('kbnij,kbnjr->kbir', tile_values, picked, preferred_element_ty...]
    ppermute x2 -> x0, starting transfers between devices: 6.14 us -> none  [the longest x1 4.85 us: extended(): before = lax.ppermute(last, axis, up)]
    gather x4 -> x0, local copies, waits for them, and re-layouts: 5.32 us -> none  [the longest x2 3.87 us: local(): picked = jnp.take(panels, col_index - first_block, axis=0)]
    ppermute x2 -> x0, waiting for transfers between devices: 3.54 us -> none  [the longest x1 3.54 us: extended(): after = lax.ppermute(first, axis, down)]
    unnamed x10 -> x2, local copies, waits for them, and re-layouts: 3.44 us -> 3.14 us
  transfers between devices with their start and end apart: 4 -> 0, of which waited for: 2 -> 0; matrix products, arithmetic and copies ran while one was open for 21% -> 0% of each run, Pallas kernels for 0% -> 0%
where the time goes in v1:
time: 39.5 us; the launch traced here: 39.3 us
  Pallas kernels  34.8 us (88%)
  local copies, waits for them, and re-layouts  3.14 us (8%)
  between operations  1.29 us (3%)
    pallas_call x1, Pallas kernels, local(): pl.pallas_call(functools.partial(kernel, n), out_shape=(jax.ShapeDtypeStr...  34.8 us
    unnamed x2, local copies, waits for them, and re-layouts  3.14 us

profile of v1, /device:TPU:0, one launch (start us, length us, event | category | flops | bytes accessed | tf_op | source)
XLA Modules:
  0.0 39.3 jit_solution(14655485004870032267)
XLA Ops:
  1.3 34.8 %projection.1 = (bf16[64,512]{1,0:T(8,128)(2,1)}, f32[4,128,128]{2,1,0:T(8,128)}) custom-call(bf16[512,128]{1,0:T(8,128)(2,1)} %snap_ref.1, s32[1,512]{1,0:T(1,128)} %bitcast.3, bf16[4,2,4,256,256]{4,3,2,1,0:T(8,128)(2,1)} %tiles_ref.1, f32[4,512]{1,0:T(4,128)} %coef_ref.1, s32[4,2,4]{2,1,0:T(2,128)} %col_ref.1, f32[1]{0:T(128)S(6)} %copy.10.freq_ref), custom_call_target="tpu_custom_call" | custom-call | tf_op jit(solution)/shard_map/projection/pallas_call | solution.py:284
  36.1 1.5 %copy.11 = bf16[512,64]{0,1:T(8,128)(2,1)} copy(bf16[512,64]{0,1:T(8,128)(2,1)} %bitcast.2) | data formatting | bytes 131072
  37.6 1.7 %copy.12 = f32[4,128,128]{2,1,0:T(8,128)} copy(f32[4,128,128]{2,1,0:T(8,128)} %get-tuple-element.9) | data formatting | bytes 524288

commit v2 on v1

--- a/solution.py
+++ b/solution.py
@@ -59,7 +59,7 @@
 def kernel(
     n, snap_ref, order_ref, tiles_ref, coef_ref, col_ref, freq_ref,
     sampled_ref, projected_ref,
-    tiles, panels, acc, gsend, grecv, gsum, gall, w, wt, psend, precv, tsend, tall, wsend, wrecv,
+    tiles, panels, acc, gsend, grecv, gsum, gall, w, terms, psend, precv, tsend, tall, wsend, wrecv,
     tile_sem, gs_sem, gr_sem, as_sem, ar_sem, hs_sem, hr_sem, fs_sem, fr_sem,
     ps_sem, pr_sem, ts_sem, tr_sem, ws_sem, wr_sem,
 ):
@@ -206,42 +206,49 @@
         image = jnp.concatenate(parts, axis=0)
         weight = jnp.where(half == 0, weights[k], weights[k + ops])
         weighted = weighted + weight * image.astype(F32)
-        psend[k] = jnp.dot(ordered_b, image, preferred_element_type=F32)
+        terms[k] = jnp.dot(ordered_b, image, preferred_element_type=F32)
     wsend[...] = weighted
-
-    def projection_part(slot, source, peer):
-        return pltpu.make_async_remote_copy(
-            src_ref=psend.at[peer // per_op], dst_ref=precv.at[source],
-            send_sem=ps_sem.at[slot], recv_sem=pr_sem.at[source],
-            device_id={"rows": peer}, device_id_type=MESH)
-
-    peers(lambda d, peer: projection_part(d, me, peer).start())
     swap = pltpu.make_async_remote_copy(
         src_ref=wsend, dst_ref=wrecv, send_sem=ws_sem, recv_sem=wr_sem,
         device_id={"coef": other}, device_id_type=MESH)
     swap.start()
-    precv[me] = psend[me // per_op]
 
     peers(lambda d, peer: gram_all(d, peer, peer).wait_recv())
     inverse_factor(jnp.concatenate([gall[i] for i in range(n)], axis=0), w)
-    for i in range(per_op):
-        wt[i] = w[i * t_rows : (i + 1) * t_rows, :]
+
+    inverse = w[...]
+    inner = jnp.dot(
+        inverse, jnp.concatenate([terms[k] for k in range(ops)], axis=1),
+        preferred_element_type=F32, precision=HIGHEST)
+    for k in range(ops):
+        projected = lax.dot_general(
+            inner[:, k * rank : (k + 1) * rank], inverse, (((1,), (1,)), ((), ())),
+            preferred_element_type=F32, precision=HIGHEST)
+        for h in range(per_op):
+            psend[k * per_op + h] = projected[h * t_rows : (h + 1) * t_rows].astype(psend.dtype)
+
+    def projection_part(slot, source, peer):
+        return pltpu.make_async_remote_copy(
+            src_ref=psend.at[peer], dst_ref=precv.at[source],
+            send_sem=ps_sem.at[slot], recv_sem=pr_sem.at[source],
+            device_id={"rows": peer}, device_id_type=MESH)
+
+    peers(lambda d, peer: projection_part(d, me, peer).start())
+    precv[me] = psend[me]
 
     swap.wait()
     both = (wsend[...] + wrecv[...]).T
     width = rank // 2
-    sampled_ref[...] = jnp.where(half == 0, both[:width], both[width:]).astype(jnp.bfloat16)
+    sampled_ref[...] = jnp.where(half == 0, both[:width], both[width:])
 
     peers(lambda d, peer: projection_part(d, peer, peer).wait_recv())
-    total = precv[0]
+    total = precv[0].astype(F32)
     if n <= 8:
         for i in range(1, n):
-            total = total + precv[i]
+            total = total + precv[i].astype(F32)
     else:
-        total = lax.fori_loop(1, n, lambda i, t: t + precv[i], total)
-    inner = jnp.dot(wt[lax.rem(me, per_op)], total, preferred_element_type=F32, precision=HIGHEST)
-    tsend[...] = lax.dot_general(
-        inner, w[...], (((1,), (1,)), ((), ())), preferred_element_type=F32, precision=HIGHEST)
+        total = lax.fori_loop(1, n, lambda i, t: t + precv[i].astype(F32), total)
+    tsend[...] = total.astype(tsend.dtype)
     tall[me] = tsend[...]
 
     def result_part(slot, source, peer):
@@ -268,9 +275,7 @@
         down.wait_send()
 
     peers(lambda d, peer: result_part(d, peer, peer).wait_recv())
-    for i in range(n):
-        k, h = divmod(i, per_op)
-        projected_ref[k, h * t_rows : (h + 1) * t_rows, :] = tall[i]
+    projected_ref[...] = tall[...]
     peers(lambda d, peer: result_part(d, me, peer).wait_send())
 
 
@@ -278,14 +283,15 @@
     slab, rank = snapshots.shape
     ops, blocks, per_row, tile_rows = tile_values.shape[:4]
     t_rows = rank * ops // n
+    wire = jnp.bfloat16 if t_rows % 16 == 0 else F32
     vmem = pl.BlockSpec(memory_space=pltpu.VMEM)
     smem = pl.BlockSpec(memory_space=pltpu.SMEM)
     dma = pltpu.SemaphoreType.DMA
     sampled_t, projected = pl.pallas_call(
         functools.partial(kernel, n),
         out_shape=(
-            jax.ShapeDtypeStruct((rank // 2, slab), jnp.bfloat16),
-            jax.ShapeDtypeStruct((ops, rank, rank), F32),
+            jax.ShapeDtypeStruct((rank // 2, slab), F32),
+            jax.ShapeDtypeStruct((n, t_rows, rank), wire),
         ),
         in_specs=[vmem, vmem, pl.BlockSpec(memory_space=pl.ANY), vmem, smem, smem],
         out_specs=(vmem, vmem),
@@ -298,11 +304,11 @@
             pltpu.VMEM((rank // n, rank), F32),
             pltpu.VMEM((n, rank // n, rank), F32),
             pltpu.VMEM((rank, rank), F32),
-            pltpu.VMEM((n // ops, t_rows, rank), F32),
             pltpu.VMEM((ops, rank, rank), F32),
-            pltpu.VMEM((n, rank, rank), F32),
-            pltpu.VMEM((t_rows, rank), F32),
-            pltpu.VMEM((n, t_rows, rank), F32),
+            pltpu.VMEM((n, t_rows, rank), wire),
+            pltpu.VMEM((n, t_rows, rank), wire),
+            pltpu.VMEM((t_rows, rank), wire),
+            pltpu.VMEM((n, t_rows, rank), wire),
             pltpu.VMEM((slab, rank), F32),
             pltpu.VMEM((slab, rank), F32),
             dma((ops,)), dma((n,)), dma((n,)), dma((n,)), dma((n,)),
@@ -313,7 +319,7 @@
             collective_id=0, has_side_effects=True, vmem_limit_bytes=58 * 1024 * 1024),
         name="projection",
     )(snapshots, panel_order.reshape(1, slab), tile_values, self_coef, col_index, frequency)
-    return sampled_t.T, projected
+    return sampled_t.T.astype(jnp.bfloat16), projected.reshape(ops, rank, rank).astype(F32)
 
 
 def solution(mesh):

time: 39.5 us -> 35.5 us (0.90)
  Pallas kernels: 34.8 us -> 30.9 us
  other arithmetic: 0 us -> 3.17 us
  local copies, waits for them, and re-layouts: 3.14 us -> 0 us
    pallas_call x1, Pallas kernels: 34.8 us -> 30.9 us  [local(): pl.pallas_call(functools.partial(kernel, n), out_shape=(jax.ShapeDtypeStr...]
    convert_element_type x0 -> x2, other arithmetic: none -> 3.17 us  [the longest x1 1.62 us: local(): projected.reshape(ops, rank, rank).astype(F32)]
    unnamed x2 -> x0, local copies, waits for them, and re-layouts: 3.14 us -> none
where the time goes in v2:
time: 35.5 us; the launch traced here: 35.4 us
  Pallas kernels  30.9 us (87%)
  other arithmetic  3.17 us (9%)
  between operations  1.29 us (4%)
    pallas_call x1, Pallas kernels, local(): pl.pallas_call(functools.partial(kernel, n), out_shape=(jax.ShapeDtypeStr...  30.9 us
    convert_element_type x1, other arithmetic, local(): projected.reshape(ops, rank, rank).astype(F32)  1.62 us
    convert_element_type x1, other arithmetic, local(): sampled_t.T.astype(jnp.bfloat16)  1.54 us

profile of v2, /device:TPU:0, one launch (start us, length us, event | category | flops | bytes accessed | tf_op | source)
XLA Modules:
  0.0 35.4 jit_solution(3694642562740639085)
XLA Ops:
  1.3 30.9 %projection.1 = (f32[64,512]{1,0:T(8,128)}, bf16[8,64,128]{2,1,0:T(8,128)(2,1)}) custom-call(bf16[512,128]{1,0:T(8,128)(2,1)} %snap_ref.1, s32[1,512]{1,0:T(1,128)} %bitcast.8, bf16[4,2,4,256,256]{4,3,2,1,0:T(8,128)(2,1)} %tiles_ref.1, f32[4,512]{1,0:T(4,128)} %coef_ref.1, s32[4,2,4]{2,1,0:T(2,128)} %col_ref.1, f32[1]{0:T(128)S(6)} %copy.8.freq_ref), custom_call_target="tpu_custom_call" | custom-call | tf_op jit(solution)/shard_map/projection/pallas_call | solution.py:290
  32.2 1.5 %convert_bitcast_fusion = bf16[512,64]{0,1:T(8,128)(2,1)} fusion(f32[64,512]{1,0:T(8,128)} %get-tuple-element.4), kind=kLoop, calls=%fused_computation.1 | loop fusion | flops 32768 | bytes 196608 | tf_op jit(solution)/shard_map/convert_element_type | solution.py:322
  33.7 1.6 %bitcast_convert_fusion = f32[4,128,128]{2,1,0:T(8,128)} fusion(bf16[4,128,128]{2,1,0:T(8,128)(2,1)} %bitcast.7), kind=kLoop, calls=%fused_computation | loop fusion | flops 65536 | bytes 393216 | tf_op jit(solution)/shard_map/convert_element_type | solution.py:322

commit v3 on v2

--- a/solution.py
+++ b/solution.py
@@ -94,16 +94,26 @@
     snap = snap_ref[...]
     snap_t = snap.astype(F32).T.astype(jnp.bfloat16)
     gram = jnp.dot(snap_t, snap, preferred_element_type=F32)
+    g_rows = rank // n
+    for i in range(n):
+        gsend[i] = gram[i * g_rows : (i + 1) * g_rows]
+
+    pl.semaphore_wait(barrier, n)
+
+    def gram_part(slot, source, peer):
+        return pltpu.make_async_remote_copy(
+            src_ref=gsend.at[peer], dst_ref=grecv.at[source],
+            send_sem=gs_sem.at[slot], recv_sem=gr_sem.at[source],
+            device_id={"rows": peer}, device_id_type=MESH)
+
+    peers(lambda d, peer: gram_part(d, me, peer).start())
+
     place = lax.broadcasted_iota(jnp.int32, (slab, slab), 0)
     one_hot = jnp.where(place == order_ref[...], 1.0, 0.0).astype(jnp.bfloat16)
     ordered_t = jnp.dot(snap_t, one_hot, preferred_element_type=F32)
     ordered = ordered_t.T
     for b in range(blocks):
         panels[blocks + b] = ordered[b * tile_rows : (b + 1) * tile_rows].astype(jnp.bfloat16)
-    g_rows = rank // n
-    for i in range(n):
-        gsend[i] = gram[i * g_rows : (i + 1) * g_rows]
-
     @pl.when(me == 0)
     def _():
         for b in range(blocks):
@@ -113,16 +123,6 @@
     def _():
         for b in range(blocks):
             panels[2 * blocks + b] = jnp.zeros(panels.shape[1:], panels.dtype)
-
-    pl.semaphore_wait(barrier, n)
-
-    def gram_part(slot, source, peer):
-        return pltpu.make_async_remote_copy(
-            src_ref=gsend.at[peer], dst_ref=grecv.at[source],
-            send_sem=gs_sem.at[slot], recv_sem=gr_sem.at[source],
-            device_id={"rows": peer}, device_id_type=MESH)
-
-    peers(lambda d, peer: gram_part(d, me, peer).start())
 
     share = blocks // 2
     mine = half * share
@@ -216,24 +216,28 @@
     peers(lambda d, peer: gram_all(d, peer, peer).wait_recv())
     inverse_factor(jnp.concatenate([gall[i] for i in range(n)], axis=0), w)
 
+    def projection_part(slot, source, peer):
+        return pltpu.make_async_remote_copy(
+            src_ref=psend.at[peer], dst_ref=precv.at[source],
+            send_sem=ps_sem.at[slot], recv_sem=pr_sem.at[source],
+            device_id={"rows": peer}, device_id_type=MESH)
+
     inverse = w[...]
-    inner = jnp.dot(
-        inverse, jnp.concatenate([terms[k] for k in range(ops)], axis=1),
-        preferred_element_type=F32, precision=HIGHEST)
-    for k in range(ops):
+    for s in range(1, ops + 1):
+        k = lax.rem(me // per_op + s, ops)
+        inner = jnp.dot(inverse, terms[k], preferred_element_type=F32, precision=HIGHEST)
         projected = lax.dot_general(
-            inner[:, k * rank : (k + 1) * rank], inverse, (((1,), (1,)), ((), ())),
+            inner, inverse, (((1,), (1,)), ((), ())),
             preferred_element_type=F32, precision=HIGHEST)
         for h in range(per_op):
             psend[k * per_op + h] = projected[h * t_rows : (h + 1) * t_rows].astype(psend.dtype)
-
-    def projection_part(slot, source, peer):
-        return pltpu.make_async_remote_copy(
-            src_ref=psend.at[peer], dst_ref=precv.at[source],
-            send_sem=ps_sem.at[slot], recv_sem=pr_sem.at[source],
-            device_id={"rows": peer}, device_id_type=MESH)
-
-    peers(lambda d, peer: projection_part(d, me, peer).start())
+        for h in range(per_op):
+            peer = k * per_op + h
+
+            @pl.when(peer != me)
+            def _():
+                projection_part(peer, me, peer).start()
+
     precv[me] = psend[me]
 
     swap.wait()
@@ -262,7 +266,7 @@
     def sent(d, peer):
         gram_part(d, me, peer).wait_send()
         gram_all(d, me, peer).wait_send()
-        projection_part(d, me, peer).wait_send()
+        projection_part(peer, me, peer).wait_send()
 
     peers(sent)
 
@@ -277,6 +281,11 @@
     peers(lambda d, peer: result_part(d, peer, peer).wait_recv())
     projected_ref[...] = tall[...]
     peers(lambda d, peer: result_part(d, me, peer).wait_send())
+
+
+def finish(sampled_ref, projected_ref, sampled_out, projected_out):
+    sampled_out[...] = sampled_ref[...].astype(sampled_out.dtype)
+    projected_out[...] = projected_ref[...].astype(projected_out.dtype)
 
 
 def local(n, snapshots, panel_order, tile_values, self_coef, col_index, frequency):
@@ -319,7 +328,15 @@
             collective_id=0, has_side_effects=True, vmem_limit_bytes=58 * 1024 * 1024),
         name="projection",
     )(snapshots, panel_order.reshape(1, slab), tile_values, self_coef, col_index, frequency)
-    return sampled_t.T.astype(jnp.bfloat16), projected.reshape(ops, rank, rank).astype(F32)
+    sampled_t, projected = pl.pallas_call(
+        finish,
+        out_shape=(
+            jax.ShapeDtypeStruct(sampled_t.shape, jnp.bfloat16),
+            jax.ShapeDtypeStruct(projected.shape, F32),
+        ),
+        name="finish",
+    )(sampled_t, projected)
+    return sampled_t.T, projected.reshape(ops, rank, rank)
 
 
 def solution(mesh):

time: 35.5 us -> 34 us (0.958)
  other arithmetic: 3.17 us -> 0 us
  Pallas kernels: 30.9 us -> 32.6 us
    convert_element_type x2 -> x0, other arithmetic: 3.17 us -> none  [the longest x1 1.62 us: local(): projected.reshape(ops, rank, rank).astype(F32)]
    pallas_call x0 -> x1, Pallas kernels: none -> 1.7 us  [local(): pl.pallas_call(finish, out_shape=(jax.ShapeDtypeStruct(sampled_t.shape, j...]
where the time goes in v3:
time: 34 us; the launch traced here: 33.8 us
  Pallas kernels  32.6 us (96%)
  between operations  1.29 us (4%)
    pallas_call x1, Pallas kernels, local(): pl.pallas_call(functools.partial(kernel, n), out_shape=(jax.ShapeDtypeStr...  30.9 us
    pallas_call x1, Pallas kernels, local(): pl.pallas_call(finish, out_shape=(jax.ShapeDtypeStruct(sampled_t.shape, j...  1.7 us

profile of v3, /device:TPU:0, one launch (start us, length us, event | category | flops | bytes accessed | tf_op | source)
XLA Modules:
  0.0 33.8 jit_solution(17594039014184268365)
XLA Ops:
  1.3 30.9 %projection.1 = (f32[64,512]{1,0:T(8,128)}, bf16[8,64,128]{2,1,0:T(8,128)(2,1)}) custom-call(bf16[512,128]{1,0:T(8,128)(2,1)} %snap_ref.1, s32[1,512]{1,0:T(1,128)} %bitcast.3, bf16[4,2,4,256,256]{4,3,2,1,0:T(8,128)(2,1)} %tiles_ref.1, f32[4,512]{1,0:T(4,128)} %coef_ref.1, s32[4,2,4]{2,1,0:T(2,128)} %col_ref.1, f32[1]{0:T(128)S(6)} %copy.8.freq_ref), custom_call_target="tpu_custom_call" | custom-call | tf_op jit(solution)/shard_map/projection/pallas_call | solution.py:299
  32.1 1.7 %finish.1 = (bf16[64,512]{1,0:T(8,128)(2,1)}, f32[8,64,128]{2,1,0:T(8,128)}) custom-call(f32[64,512]{1,0:T(8,128)} %get-tuple-element.6.sampled_ref, bf16[8,64,128]{2,1,0:T(8,128)(2,1)} %get-tuple-element.7.projected_ref), custom_call_target="tpu_custom_call" | custom-call | tf_op jit(solution)/shard_map/finish/pallas_call | solution.py:331

commit v4 on v3

--- a/solution.py
+++ b/solution.py
@@ -224,20 +224,15 @@
 
     inverse = w[...]
     for s in range(1, ops + 1):
-        k = lax.rem(me // per_op + s, ops)
+        k = s - 1
         inner = jnp.dot(inverse, terms[k], preferred_element_type=F32, precision=HIGHEST)
         projected = lax.dot_general(
             inner, inverse, (((1,), (1,)), ((), ())),
             preferred_element_type=F32, precision=HIGHEST)
         for h in range(per_op):
             psend[k * per_op + h] = projected[h * t_rows : (h + 1) * t_rows].astype(psend.dtype)
-        for h in range(per_op):
-            peer = k * per_op + h
-
-            @pl.when(peer != me)
-            def _():
-                projection_part(peer, me, peer).start()
-
+
+    peers(lambda d, peer: projection_part(peer, me, peer).start())
     precv[me] = psend[me]
 
     swap.wait()

time: 34 us -> 34.3 us (level)
  no operation moved by 1% of the time
where the time goes in v4:
time: 34.3 us; the launch traced here: 34.1 us
  Pallas kernels  32.9 us (96%)
  between operations  1.29 us (4%)
    pallas_call x1, Pallas kernels, local(): pl.pallas_call(functools.partial(kernel, n), out_shape=(jax.ShapeDtypeStr...  31.2 us
    pallas_call x1, Pallas kernels, local(): pl.pallas_call(finish, out_shape=(jax.ShapeDtypeStruct(sampled_t.shape, j...  1.7 us

profile of v4, /device:TPU:0, one launch (start us, length us, event | category | flops | bytes accessed | tf_op | source)
XLA Modules:
  0.0 34.1 jit_solution(3716194508714873657)
XLA Ops:
  1.3 31.2 %projection.1 = (f32[64,512]{1,0:T(8,128)}, bf16[8,64,128]{2,1,0:T(8,128)(2,1)}) custom-call(bf16[512,128]{1,0:T(8,128)(2,1)} %snap_ref.1, s32[1,512]{1,0:T(1,128)} %bitcast.3, bf16[4,2,4,256,256]{4,3,2,1,0:T(8,128)(2,1)} %tiles_ref.1, f32[4,512]{1,0:T(4,128)} %coef_ref.1, s32[4,2,4]{2,1,0:T(2,128)} %col_ref.1, f32[1]{0:T(128)S(6)} %copy.8.freq_ref), custom_call_target="tpu_custom_call" | custom-call | tf_op jit(solution)/shard_map/projection/pallas_call | solution.py:294
  32.4 1.7 %finish.1 = (bf16[64,512]{1,0:T(8,128)(2,1)}, f32[8,64,128]{2,1,0:T(8,128)}) custom-call(f32[64,512]{1,0:T(8,128)} %get-tuple-element.6.sampled_ref, bf16[8,64,128]{2,1,0:T(8,128)(2,1)} %get-tuple-element.7.projected_ref), custom_call_target="tpu_custom_call" | custom-call | tf_op jit(solution)/shard_map/finish/pallas_call | solution.py:326
